TPU v7x, 32 devices: a whole 2x2x4 slice. The times are simulated.
32 devices in a mesh: grp: 2 (over x), uly: 8 (over z, y), blk: 2 (over core).
Axes of the slice: x: 2, y: 2, z: 4, core: 2. Of those that a mesh axis runs over, the one named last changes fastest.
Arguments:
- queries: bfloat16 [8192, 8, 128], P(('grp', 'uly', 'blk')), parts along dimension 0, may hold values from -8 to 8
- keys: bfloat16 [8192, 8, 128], P(('grp', 'uly', 'blk')), parts along dimension 0, may hold values from -8 to 8
- values: bfloat16 [8192, 8, 128], P(('grp', 'uly', 'blk')), parts along dimension 0, may hold values from -6 to 6
- pattern: int32 [16, 32, 8], P(('grp', 'uly')), parts along dimension 0, may hold values from 0 to 31, as said below
- heavy: int32 [16, 2], P(('grp', 'uly')), parts along dimension 0, may hold values from 0 to 31, as said below
Outputs:
- attended: bfloat16 [8192, 8, 128], P(('grp', 'uly', 'blk')), parts along dimension 0
There are 2 independent parts, one for each index of `grp`. A program takes and returns all parts, laid end to end along the dimension named above; each array names one. Nothing has to cross between parts.
Inputs may be any that keep to these rules, and one draw needn't show every extreme that they name: `pattern`: row t of each head lists 8 distinct tiles, the first of them t itself. `heavy`: each head lists 2 distinct tiles.
All inputs are finite; a program needn't handle non-finite values.
Results may differ from a plain program's by a relative error of at most 0.0075.
Values may be sent and summed in bfloat16 or wider, within the bound.
A program may use at most 64 MiB of HBM per device.

v0:
```python
import math

import jax
import jax.numpy as jnp
from jax import lax
from jax.sharding import PartitionSpec as P

TILE = 128


def from_behind(x, axis, by):
    devices = lax.axis_size(axis)
    return lax.ppermute(x, axis, [(i, (i + by) % devices) for i in range(devices)])


def attend(query_rows, key_rows, value_rows):
    scores = jnp.einsum(
        "gqd,gkd->gqk", query_rows, key_rows, preferred_element_type=jnp.float32
    ) * query_rows.shape[-1] ** (-0.5)
    row_max = jnp.max(scores, axis=-1, keepdims=True)
    weights = jnp.exp(scores - row_max)
    row_total = jnp.sum(weights, axis=-1, keepdims=True)
    probabilities = weights.astype(jnp.bfloat16)
    blended = jnp.einsum(
        "gqk,gkd->gqd", probabilities, value_rows, preferred_element_type=jnp.float32
    )
    return (blended / row_total).astype(jnp.bfloat16)


def per_device(queries, keys, values, pattern, heavy):
    local_tokens = queries.shape[0]
    ulysses = lax.axis_size("uly")
    half_index = lax.axis_index("blk")
    per_shard = local_tokens // TILE
    near_q, near_k, near_v = (
        lax.all_to_all(queries, "uly", split_axis=1, concat_axis=0, tiled=True),
        lax.all_to_all(keys, "uly", split_axis=1, concat_axis=0, tiled=True),
        lax.all_to_all(values, "uly", split_axis=1, concat_axis=0, tiled=True),
    )
    far_k, far_v = from_behind((near_k, near_v), "blk", 1)

    def in_order(near, far):
        lower = jnp.where(half_index == 0, near, far)
        upper = jnp.where(half_index == 0, far, near)
        shape_rest = near.shape[1:]
        paired = jnp.stack(
            [
                lower.reshape((ulysses, local_tokens) + shape_rest),
                upper.reshape((ulysses, local_tokens) + shape_rest),
            ],
            axis=1,
        )
        return paired.reshape((2 * near.shape[0],) + shape_rest)

    full_keys = in_order(near_k, far_k)
    full_values = in_order(near_v, far_v)
    head_size = queries.shape[2]
    tile_count = near_q.shape[0] // TILE
    local_ids = jnp.arange(tile_count, dtype=jnp.int32)
    global_ids = (local_ids // per_shard * 2 + half_index) * per_shard + local_ids % per_shard
    group = math.gcd(tile_count, max(1, 512 // TILE))
    group_count = tile_count // group
    listed = pattern.shape[2]
    query_tiles = near_q[:, 0].reshape(tile_count, TILE, head_size)
    key_all = full_keys[:, 0]
    value_all = full_values[:, 0]
    key_tiles = key_all.reshape(-1, TILE, head_size)
    value_tiles = value_all.reshape(-1, TILE, head_size)
    chosen = pattern[0][global_ids]

    def sparse_group(inputs):
        query_group, index_group = inputs
        return attend(
            query_group,
            key_tiles[index_group].reshape(group, listed * TILE, head_size),
            value_tiles[index_group].reshape(group, listed * TILE, head_size),
        )

    sparse_out = lax.map(
        sparse_group,
        (
            query_tiles.reshape(group_count, group, TILE, head_size),
            chosen.reshape(group_count, group, listed),
        ),
    )
    sparse_out = sparse_out.reshape(tile_count, TILE, head_size)

    def dense_tile(query_tile):
        return attend(query_tile[None], key_all[None], value_all[None])[0]

    heavy_ids = heavy[0]
    owner = heavy_ids // per_shard % 2
    position = heavy_ids // (2 * per_shard) * per_shard + heavy_ids % per_shard
    mine_rows = jnp.where(
        (owner == half_index)[:, None, None], query_tiles[position], jnp.zeros((), jnp.bfloat16)
    )
    heavy_rows = mine_rows + from_behind(mine_rows, "blk", 1)
    paired_rows = heavy_rows.reshape(-1, 2, TILE, head_size)
    my_share = lax.dynamic_index_in_dim(paired_rows, half_index, axis=1, keepdims=False)
    finished = lax.map(dense_tile, my_share)
    partner_done = from_behind(finished, "blk", 1)
    results = jnp.where(
        half_index == 0,
        jnp.stack([finished, partner_done], axis=1),
        jnp.stack([partner_done, finished], axis=1),
    )
    results = results.reshape(-1, TILE, head_size)
    target = jnp.where(owner == half_index, position, tile_count)
    sparse_out = sparse_out.at[target].set(results, mode="drop")
    outputs = [sparse_out.reshape(tile_count * TILE, head_size)]
    local_out = jnp.stack(outputs, axis=1)
    return lax.all_to_all(local_out, "uly", split_axis=0, concat_axis=1, tiled=True)


def solution(mesh):
    placed = (
        P(("grp", "uly", "blk"), None, None),
        P(("grp", "uly", "blk"), None, None),
        P(("grp", "uly", "blk"), None, None),
        P(("grp", "uly"), None, None),
        P(("grp", "uly"), None),
    )
    return jax.shard_map(
        per_device,
        mesh=mesh,
        in_specs=placed,
        out_specs=P(("grp", "uly", "blk"), None, None),
        check_vma=False,
    )
```

profile of v0, /device:TPU:0, one launch (start us, length us, event | category | flops | bytes accessed | tf_op | source)
XLA Modules:
  0.0 126.6 jit_solution(5132518003359706949)
XLA Ops:
  0.0 2.0 %copy.35 = bf16[256,8,128]{2,0,1:T(8,128)(2,1)} copy(bf16[256,8,128]{2,1,0:T(8,128)(2,1)} %param.8) | data formatting | bytes 1048576 | tf_op args[1]
  2.0 7.3 %all-to-all-start.1 = ((bf16[256,8,128]{2,0,1:T(8,128)(2,1)}), bf16[256,8,128]{2,0,1:T(8,128)(2,1)S(1)}, u32[]{:S(2)}, u32[]{:S(2)}) async-start(bf16[256,8,128]{2,0,1:T(8,128)(2,1)} %copy.35), calls=%async_computation.1 | async-start | bytes 1048576 | tf_op jit(solution)/shard_map/all_to_all | solution.py:37
  10.2 13.6 %all-to-all-done.1 = bf16[256,8,128]{2,0,1:T(8,128)(2,1)S(1)} async-done(((bf16[256,8,128]{2,0,1:T(8,128)(2,1)}), bf16[256,8,128]{2,0,1:T(8,128)(2,1)S(1)}, u32[]{:S(2)}, u32[]{:S(2)}) %all-to-all-start.1) | async-done | bytes 524320 | tf_op jit(solution)/shard_map/all_to_all | solution.py:37
  23.8 3.6 %all-to-all-start.2 = ((bf16[256,8,128]{2,0,1:T(8,128)(2,1)}), bf16[256,8,128]{2,0,1:T(8,128)(2,1)S(1)}, u32[]{:S(2)}, u32[]{:S(2)}) async-start(bf16[256,8,128]{2,0,1:T(8,128)(2,1)} %copy.38), calls=%async_computation.2 | async-start | bytes 1048576 | tf_op jit(solution)/shard_map/all_to_all | solution.py:38
  28.3 13.8 %all-to-all-done.2 = bf16[256,8,128]{2,0,1:T(8,128)(2,1)S(1)} async-done(((bf16[256,8,128]{2,0,1:T(8,128)(2,1)}), bf16[256,8,128]{2,0,1:T(8,128)(2,1)S(1)}, u32[]{:S(2)}, u32[]{:S(2)}) %all-to-all-start.2) | async-done | bytes 524320 | tf_op jit(solution)/shard_map/all_to_all | solution.py:38
  42.1 4.2 %all-to-all-start = ((bf16[256,8,128]{2,0,1:T(8,128)(2,1)}), bf16[256,8,128]{2,0,1:T(8,128)(2,1)}, u32[]{:S(2)}, u32[]{:S(2)}) async-start(bf16[256,8,128]{2,0,1:T(8,128)(2,1)} %copy.33), calls=%async_computation | async-start | bytes 1048576 | tf_op jit(solution)/shard_map/all_to_all | solution.py:36
  47.6 12.9 %all-to-all-done = bf16[256,8,128]{2,0,1:T(8,128)(2,1)} async-done(((bf16[256,8,128]{2,0,1:T(8,128)(2,1)}), bf16[256,8,128]{2,0,1:T(8,128)(2,1)}, u32[]{:S(2)}, u32[]{:S(2)}) %all-to-all-start) | async-done | bytes 524320 | tf_op jit(solution)/shard_map/all_to_all | solution.py:36
  60.5 1.6 %gather_fusion.3 = bf16[2,128,128]{2,1,0:T(8,128)(2,1)S(1)} fusion(bf16[16,128,128]{2,1,0:T(8,128)(2,1)} %bitcast.36, s32[1024]{0:T(1024)S(1)} %pad_clamp_fusion.1), kind=kCustom, calls=%fused_computation.3 | custom fusion | bytes 131080 | tf_op jit(solution)/shard_map/gather | solution.py:95
  63.5 1.7 %fusion.35 = (f32[128]{0:T(128)S(1)}, f32[128,4096]{1,0:T(8,128)S(1)}) fusion(bf16[4096,128]{1,0:T(8,128)(2,1)} %bitcast.39, bf16[2,128,128]{2,1,0:T(8,128)(2,1)S(1)} %collective-permute-done.2, s32[]{:T(128)S(6)} %select_n.202, bf16[2,128,128]{2,1,0:T(8,128)(2,1)S(1)} %broadcast_select_fusion.4), kind=kOutput, calls=%fused_computation.85 | convolution fusion | flops 135282560 | bytes 3211780 | tf_op jit(solution)/shard_map/while/body/eval_jaxpr/gqd,gkd->gqk/dot_general | solution.py:17
  66.9 35.4 %while.2 = (s32[]{:T(128)}, bf16[4,4,128,128]{3,2,1,0:T(8,128)(2,1)}, bf16[4,4,128,128]{3,2,1,0:T(8,128)(2,1)}, s32[4,4,8]{2,1,0:T(4,128)S(1)}, bf16[32,128,128]...) while((s32[]{:T(128)}, bf16[4,4,128,128]{3,2,1,0:T(8,128)(2,1)}, ...), condition=%wide.region_3.4_spmd, body=%wide.region_0.3_spmd.sunk | while | flops 272760928 | bytes 17055724 | solution.py:79
  67.0 2.0 %gather_fusion.1 = bf16[32,128,128]{2,1,0:T(8,128)(2,1)S(1)} fusion(bf16[32,128,128]{2,1,0:T(8,128)(2,1)} %get-tuple-element.136, s32[1024]{0:T(1024)S(1)} %pad_clamp_fusion.4), kind=kCustom, calls=%fused_computation.clone.1 | custom fusion | bytes 2097280 | tf_op jit(solution)/shard_map/while/body/eval_jaxpr/gather | solution.py:75
  71.6 1.7 %gather_fusion = bf16[32,128,128]{2,1,0:T(8,128)(2,1)} fusion(bf16[32,128,128]{2,1,0:T(8,128)(2,1)S(1)} %copy-done.1, s32[1024]{0:T(1024)S(1)} %pad_clamp_fusion.4), kind=kCustom, calls=%fused_computation.1.clone.1 | custom fusion | bytes 2097280 | tf_op jit(solution)/shard_map/while/body/eval_jaxpr/gather | solution.py:76
  73.3 2.5 %fusion.49 = bf16[4,4,128,128]{3,2,1,0:T(8,128)(2,1)} fusion(bf16[4,4,128,128]{3,2,1,0:T(8,128)(2,1)} %get-tuple-element.126, s32[]{:T(128)} %get-tuple-element.125, bf16[4,1024,128]{2,1,0:T(8,128)(2,1)} %bitcast.131, f32[4,128,1024]{2,1,0:T(8,128)S(1)} %get-tuple-element.116, f32[4,128]{1,0:T(4,128)S(1)} %get-tuple-element.117, ...), kind=kOutput, calls=%fused_computation.12.clone.1 | convolution fusion | flops 135921664 | bytes 3281408 | tf_op jit(solution)/shard_map/while/body/eval_jaxpr/gqk,gkd->gqd/dot_general | solution.py:24
  75.8 2.0 %gather_fusion.1 = bf16[32,128,128]{2,1,0:T(8,128)(2,1)S(1)} fusion(bf16[32,128,128]{2,1,0:T(8,128)(2,1)} %get-tuple-element.136, s32[1024]{0:T(1024)S(1)} %pad_clamp_fusion.4), kind=kCustom, calls=%fused_computation.clone.1 | custom fusion | bytes 2097280 | tf_op jit(solution)/shard_map/while/body/eval_jaxpr/gather | solution.py:75
  80.5 1.7 %gather_fusion = bf16[32,128,128]{2,1,0:T(8,128)(2,1)} fusion(bf16[32,128,128]{2,1,0:T(8,128)(2,1)S(1)} %copy-done.1, s32[1024]{0:T(1024)S(1)} %pad_clamp_fusion.4), kind=kCustom, calls=%fused_computation.1.clone.1 | custom fusion | bytes 2097280 | tf_op jit(solution)/shard_map/while/body/eval_jaxpr/gather | solution.py:76
  82.2 2.5 %fusion.49 = bf16[4,4,128,128]{3,2,1,0:T(8,128)(2,1)} fusion(bf16[4,4,128,128]{3,2,1,0:T(8,128)(2,1)} %get-tuple-element.126, s32[]{:T(128)} %get-tuple-element.125, bf16[4,1024,128]{2,1,0:T(8,128)(2,1)} %bitcast.131, f32[4,128,1024]{2,1,0:T(8,128)S(1)} %get-tuple-element.116, f32[4,128]{1,0:T(4,128)S(1)} %get-tuple-element.117, ...), kind=kOutput, calls=%fused_computation.12.clone.1 | convolution fusion | flops 135921664 | bytes 3281408 | tf_op jit(solution)/shard_map/while/body/eval_jaxpr/gqk,gkd->gqd/dot_general | solution.py:24
  84.7 2.0 %gather_fusion.1 = bf16[32,128,128]{2,1,0:T(8,128)(2,1)S(1)} fusion(bf16[32,128,128]{2,1,0:T(8,128)(2,1)} %get-tuple-element.136, s32[1024]{0:T(1024)S(1)} %pad_clamp_fusion.4), kind=kCustom, calls=%fused_computation.clone.1 | custom fusion | bytes 2097280 | tf_op jit(solution)/shard_map/while/body/eval_jaxpr/gather | solution.py:75
  89.3 1.7 %gather_fusion = bf16[32,128,128]{2,1,0:T(8,128)(2,1)} fusion(bf16[32,128,128]{2,1,0:T(8,128)(2,1)S(1)} %copy-done.1, s32[1024]{0:T(1024)S(1)} %pad_clamp_fusion.4), kind=kCustom, calls=%fused_computation.1.clone.1 | custom fusion | bytes 2097280 | tf_op jit(solution)/shard_map/while/body/eval_jaxpr/gather | solution.py:76
  91.0 2.5 %fusion.49 = bf16[4,4,128,128]{3,2,1,0:T(8,128)(2,1)} fusion(bf16[4,4,128,128]{3,2,1,0:T(8,128)(2,1)} %get-tuple-element.126, s32[]{:T(128)} %get-tuple-element.125, bf16[4,1024,128]{2,1,0:T(8,128)(2,1)} %bitcast.131, f32[4,128,1024]{2,1,0:T(8,128)S(1)} %get-tuple-element.116, f32[4,128]{1,0:T(4,128)S(1)} %get-tuple-element.117, ...), kind=kOutput, calls=%fused_computation.12.clone.1 | convolution fusion | flops 135921664 | bytes 3281408 | tf_op jit(solution)/shard_map/while/body/eval_jaxpr/gqk,gkd->gqd/dot_general | solution.py:24
  93.6 2.0 %gather_fusion.1 = bf16[32,128,128]{2,1,0:T(8,128)(2,1)S(1)} fusion(bf16[32,128,128]{2,1,0:T(8,128)(2,1)} %get-tuple-element.136, s32[1024]{0:T(1024)S(1)} %pad_clamp_fusion.4), kind=kCustom, calls=%fused_computation.clone.1 | custom fusion | bytes 2097280 | tf_op jit(solution)/shard_map/while/body/eval_jaxpr/gather | solution.py:75
  98.2 1.7 %gather_fusion = bf16[32,128,128]{2,1,0:T(8,128)(2,1)} fusion(bf16[32,128,128]{2,1,0:T(8,128)(2,1)S(1)} %copy-done.1, s32[1024]{0:T(1024)S(1)} %pad_clamp_fusion.4), kind=kCustom, calls=%fused_computation.1.clone.1 | custom fusion | bytes 2097280 | tf_op jit(solution)/shard_map/while/body/eval_jaxpr/gather | solution.py:76
  99.9 2.5 %fusion.49 = bf16[4,4,128,128]{3,2,1,0:T(8,128)(2,1)} fusion(bf16[4,4,128,128]{3,2,1,0:T(8,128)(2,1)} %get-tuple-element.126, s32[]{:T(128)} %get-tuple-element.125, bf16[4,1024,128]{2,1,0:T(8,128)(2,1)} %bitcast.131, f32[4,128,1024]{2,1,0:T(8,128)S(1)} %get-tuple-element.116, f32[4,128]{1,0:T(4,128)S(1)} %get-tuple-element.117, ...), kind=kOutput, calls=%fused_computation.12.clone.1 | convolution fusion | flops 135921664 | bytes 3281408 | tf_op jit(solution)/shard_map/while/body/eval_jaxpr/gqk,gkd->gqd/dot_general | solution.py:24
  104.3 2.0 %reduce.4 = bf16[2048,128]{1,0:T(8,128)(2,1)S(1)} reduce(bf16[2048,1,128]{2,0,1:T(8,128)(2,1)} %bitcast.142, bf16[]{:T(256)} %broadcast.507), dimensions={1}, to_apply=%copy.41.reduce_sub_computation | reduce | bytes 1048578 | tf_op jit(solution)/shard_map/stack;reshape | solution.py:111
  106.4 18.5 %all_to_all.69 = bf16[8,2,16384]{2,1,0:T(2,128)(2,1)S(1)} all-to-all(bf16[8,2,16384]{2,1,0:T(2,128)(2,1)S(1)} %reshape.468), channel_id=1, replica_groups=mesh['grp'=2,'uly'=8,'blk'=2] {'uly'}, dimensions={0} | all-to-all | bytes 1048576 | tf_op jit(solution)/shard_map/all_to_all | solution.py:112
  (70 shorter events, 20.8 us)
Async XLA Ops:
  0.0 9.3 %copy-start.2 = (bf16[256,8,128]{2,1,0:T(8,128)(2,1)S(1)}, bf16[256,8,128]{2,1,0:T(8,128)(2,1)}, u32[]{:S(2)}) copy-start(bf16[256,8,128]{2,1,0:T(8,128)(2,1)} %param.9) | copy-start | bytes 1572868
  0.0 27.4 %copy-start.3 = (bf16[256,8,128]{2,1,0:T(8,128)(2,1)S(1)}, bf16[256,8,128]{2,1,0:T(8,128)(2,1)}, u32[]{:S(2)}) copy-start(bf16[256,8,128]{2,1,0:T(8,128)(2,1)} %param.7) | copy-start | bytes 1572868
  2.0 21.8 %all-to-all-start.1 = ((bf16[256,8,128]{2,0,1:T(8,128)(2,1)}), bf16[256,8,128]{2,0,1:T(8,128)(2,1)S(1)}, u32[]{:S(2)}, u32[]{:S(2)}) async-start(bf16[256,8,128]{2,0,1:T(8,128)(2,1)} %copy.35), calls=%async_computation.1 | async-start | bytes 1048576 | tf_op jit(solution)/shard_map/all_to_all | solution.py:37
  9.3 37.0 %copy-start.4 = (s32[1,32,8]{1,2,0:T(8,128)S(1)}, s32[1,32,8]{1,2,0:T(8,128)}, u32[]{:S(2)}) copy-start(s32[1,32,8]{1,2,0:T(8,128)} %param.10) | copy-start | bytes 3076
  9.3 37.6 %copy-start.5 = (s32[1,2]{1,0:T(1,128)S(1)}, s32[1,2]{1,0:T(1,128)}, u32[]{:S(2)}) copy-start(s32[1,2]{1,0:T(1,128)} %param.11) | copy-start | bytes 28
  23.8 18.3 %all-to-all-start.2 = ((bf16[256,8,128]{2,0,1:T(8,128)(2,1)}), bf16[256,8,128]{2,0,1:T(8,128)(2,1)S(1)}, u32[]{:S(2)}, u32[]{:S(2)}) async-start(bf16[256,8,128]{2,0,1:T(8,128)(2,1)} %copy.38), calls=%async_computation.2 | async-start | bytes 1048576 | tf_op jit(solution)/shard_map/all_to_all | solution.py:38
  42.1 18.4 %all-to-all-start = ((bf16[256,8,128]{2,0,1:T(8,128)(2,1)}), bf16[256,8,128]{2,0,1:T(8,128)(2,1)}, u32[]{:S(2)}, u32[]{:S(2)}) async-start(bf16[256,8,128]{2,0,1:T(8,128)(2,1)} %copy.33), calls=%async_computation | async-start | bytes 1048576 | tf_op jit(solution)/shard_map/all_to_all | solution.py:36
  47.0 15.3 %collective-permute-start = (bf16[2048,1,128]{2,0,1:T(8,128)(2,1)S(1)}, bf16[2048,1,128]{2,0,1:T(8,128)(2,1)S(1)}, u32[]{:S(2)}, u32[]{:S(2)}) collective-permute-start(bf16[2048,1,128]{2,0,1:T(8,128)(2,1)S(1)} %bitcast.132), channel_id=1, source_target_pairs={{0,1},{1,0},{2,3},{3,2},{4,5},{5,4},{6,7},{7,6},{8,9},{9,8},{10,11... | collective-permute-start | bytes 1572872 | tf_op jit(solution)/shard_map/ppermute | solution.py:13
  47.1 15.2 %collective-permute-start.1 = (bf16[2048,1,128]{2,0,1:T(8,128)(2,1)S(1)}, bf16[2048,1,128]{2,0,1:T(8,128)(2,1)S(1)}, u32[]{:S(2)}, u32[]{:S(2)}) collective-permute-start(bf16[2048,1,128]{2,0,1:T(8,128)(2,1)S(1)} %bitcast.134), channel_id=1, source_target_pairs={{0,1},{1,0},{2,3},{3,2},{4,5},{5,4},{6,7},{7,6},{8,9},{9,8},{10,11... | collective-permute-start | bytes 1572872 | tf_op jit(solution)/shard_map/ppermute | solution.py:13
  62.2 1.3 %collective-permute-start.2 = (bf16[2,128,128]{2,1,0:T(8,128)(2,1)S(1)}, bf16[2,128,128]{2,1,0:T(8,128)(2,1)S(1)}, u32[]{:S(2)}, u32[]{:S(2)}) collective-permute-start(bf16[2,128,128]{2,1,0:T(8,128)(2,1)S(1)} %broadcast_select_fusion.4), channel_id=1, source_target_pairs={{0,1},{1,0},{2,3},{3,2},{4,5},{5,4},{6,7},{7,6},{8,9},{9,8},{10,11... | collective-permute-start | bytes 196616 | tf_op jit(solution)/shard_map/ppermute | solution.py:13
  65.8 1.1 copy-start
  66.3 36.0 %collective-permute-start.3 = (bf16[1,128,128]{2,1,0:T(8,128)(2,1)S(1)}, bf16[1,128,128]{2,1,0:T(8,128)(2,1)S(1)}, u32[]{:S(2)}, u32[]{:S(2)}) collective-permute-start(bf16[1,128,128]{2,1,0:T(8,128)(2,1)S(1)} %fusion.16), channel_id=1, source_target_pairs={{0,1},{1,0},{2,3},{3,2},{4,5},{5,4},{6,7},{7,6},{8,9},{9,8},{10,11... | collective-permute-start | bytes 98312 | tf_op jit(solution)/shard_map/ppermute | solution.py:13
  70.4 1.2 copy-start.1
  79.2 1.2 copy-start.1
  88.1 1.2 copy-start.1
  97.0 1.2 copy-start.1
where the time goes:
time: 128 us; the launch traced here: 127 us
  waiting for transfers between devices  40.3 us (31%)
  local copies, waits for them, and re-layouts  27.7 us (22%)
  blocking collectives  18.5 us (14%)
  matrix products  17.8 us (14%)
  starting transfers between devices  16.2 us (13%)
  other arithmetic  5.95 us (5%)
    all_to_all x1, blocking collectives, per_device(): lax.all_to_all(local_out, 'uly', split_axis=0, concat_axis=1, tiled=True)  18.5 us
    all_to_all x1, waiting for transfers between devices, per_device(): lax.all_to_all(values, 'uly', split_axis=1, concat_axis=0, tiled=True)  13.8 us
    all_to_all x1, waiting for transfers between devices, per_device(): lax.all_to_all(keys, 'uly', split_axis=1, concat_axis=0, tiled=True)  13.6 us
    all_to_all x1, waiting for transfers between devices, per_device(): lax.all_to_all(queries, 'uly', split_axis=1, concat_axis=0, tiled=True)  12.9 us
    dot_general x5, matrix products, attend(): jnp.einsum('gqk,gkd->gqd', probabilities, value_rows, preferred_element_t...  10.4 us
    gather x4, local copies, waits for them, and re-layouts, sparse_group(): key_tiles[index_group].reshape(group, listed * TILE, head_size)  7.89 us
    dot_general x5, matrix products, attend(): jnp.einsum('gqd,gkd->gqk', query_rows, key_rows, preferred_element_type=j...  7.44 us
    all_to_all x1, starting transfers between devices, per_device(): lax.all_to_all(keys, 'uly', split_axis=1, concat_axis=0, tiled=True)  7.28 us
  transfers between devices with their start and end apart: 7, of which 3 were waited for; matrix products, arithmetic and copies ran while one was open for 30% of the time, Pallas kernels for 0%

commit v1 on v0

v1 whole, which is shorter than its diff:
```python
import functools
import math

import jax
import jax.numpy as jnp
from jax import lax
from jax.experimental import pallas as pl
from jax.experimental.pallas import tpu as pltpu
from jax.sharding import PartitionSpec as P

TILE = 128
MESH = pl.DeviceIdType.MESH


def flip(u, d, count):
    if count & (count - 1):
        return (d + count - u) % count
    out, k = 0, 1
    while k < count:
        out = out + ((u // k + d // k) % 2) * k
        k *= 2
    return out


def kernel(
    U, per, pat, heavy, q_in, k_in, v_in, out,
    Q, K, V, probs, total, dense_p, dense_o, o_send,
    send_sem, recv_sem, fsend_sem, frecv_sem, loc_sem, osend_sem, orecv_sem,
):
    u, b = lax.axis_index("uly"), lax.axis_index("blk")
    sib = 1 - b
    tiles, head = K.shape[0], K.shape[2]
    listed, heavies = pat.shape[2], heavy.shape[1]
    c2 = head ** (-0.5) * math.log2(math.e)
    group = math.gcd(tiles, 8)
    bufs, ins = (K, Q, V), (k_in, q_in, v_in)

    barrier = pltpu.get_barrier_semaphore()

    def greet(d, c):
        pl.semaphore_signal(
            barrier, inc=1, device_id={"uly": flip(u, d, U), "blk": b}, device_id_type=MESH
        )
        return c

    lax.fori_loop(1, U, greet, 0)
    pl.semaphore_signal(barrier, inc=1, device_id={"uly": u, "blk": sib}, device_id_type=MESH)
    pl.semaphore_wait(barrier, U)

    def at(buf, s, half):
        return buf.at[pl.ds((s * 2 + half) * per, per)]

    def away(n, s):
        return pltpu.make_async_remote_copy(
            src_ref=ins[n].at[s], dst_ref=at(bufs[n], u, b),
            send_sem=send_sem.at[n, s], recv_sem=recv_sem.at[n, u],
            device_id={"uly": s, "blk": b}, device_id_type=MESH,
        )

    def arriving(n, s):
        return pltpu.make_async_remote_copy(
            src_ref=ins[n].at[s], dst_ref=at(bufs[n], s, b),
            send_sem=send_sem.at[n, s], recv_sem=recv_sem.at[n, s],
            device_id={"uly": s, "blk": b}, device_id_type=MESH,
        )

    def across(n, s):
        return pltpu.make_async_remote_copy(
            src_ref=at(bufs[n], s, b), dst_ref=at(bufs[n], s, b),
            send_sem=fsend_sem.at[n, s], recv_sem=frecv_sem.at[n, s],
            device_id={"uly": u, "blk": sib}, device_id_type=MESH,
        )

    def across_in(n, s):
        return pltpu.make_async_remote_copy(
            src_ref=at(bufs[n], s, sib), dst_ref=at(bufs[n], s, sib),
            send_sem=fsend_sem.at[n, s], recv_sem=frecv_sem.at[n, s],
            device_id={"uly": u, "blk": sib}, device_id_type=MESH,
        )

    def own(n):
        return pltpu.make_async_copy(ins[n].at[u], at(bufs[n], u, b), loc_sem.at[n])

    def own_across(n):
        return pltpu.make_async_remote_copy(
            src_ref=ins[n].at[u], dst_ref=at(bufs[n], u, b),
            send_sem=fsend_sem.at[n, u], recv_sem=frecv_sem.at[n, u],
            device_id={"uly": u, "blk": sib}, device_id_type=MESH,
        )

    for n in range(3):
        def push(i, c, n=n):
            away(n, flip(u, U - 1 - i, U)).start()
            return c

        lax.fori_loop(0, U - 1, push, 0)
        own(n).start()
        own_across(n).start()

    def relay(n, s):
        arriving(n, s).wait_recv()
        across(n, s).start()

    for n in range(2):
        def pass_on(i, c, n=n):
            relay(n, flip(u, U - 1 - i, U))
            return c

        lax.fori_loop(0, U - 1, pass_on, 0)
    for n in range(2):
        own(n).wait()

        def take(s, c, n=n):
            across_in(n, s).wait_recv()
            return c

        lax.fori_loop(0, U, take, 0)

    def scores(query, key_rows):
        return lax.dot_general(
            query, key_rows, (((1,), (1,)), ((), ())), preferred_element_type=jnp.float32
        )

    def score_tile(s, i):
        tile = (s * 2 + b) * per + i
        slot = s * per + i
        rows = jnp.concatenate([K[pat[0, tile, j]] for j in range(listed)], axis=0)
        sc = scores(Q[tile], rows)
        top = jnp.max(sc, axis=-1, keepdims=True)
        w = jnp.exp2((sc - top) * c2)
        total[slot] = jnp.broadcast_to(jnp.sum(w, axis=-1, keepdims=True), (TILE, head))
        probs[slot] = w.astype(jnp.bfloat16)

    def score_chunk(c, carry):
        s = flip(u, U - 1 - c, U)
        for i in range(per):
            score_tile(s, i)

        return carry

    def score_and_relay(c, carry):
        score_chunk(c, carry)
        relay(2, flip(u, U - 1 - c, U))
        return carry

    def dense_scores(h):
        query = Q[heavy[0, h]]

        def keys_of(g):
            return K[pl.ds(g * group, group)].reshape(group * TILE, head)

        def top_of(g, top):
            return jnp.maximum(top, jnp.max(scores(query, keys_of(g)), axis=-1, keepdims=True))

        top = lax.fori_loop(
            0, tiles // group, top_of, jnp.full((TILE, 1), -jnp.inf, jnp.float32)
        )

        def weigh(g, acc):
            w = jnp.exp2((scores(query, keys_of(g)) - top) * c2)
            dense_p[h, g] = w.astype(jnp.bfloat16)
            return acc + jnp.sum(w, axis=-1, keepdims=True)

        acc = lax.fori_loop(0, tiles // group, weigh, jnp.zeros((TILE, 1), jnp.float32))
        dense_o[h] = jnp.broadcast_to(acc, (TILE, head))

    for h in range(heavies):
        dense_scores(h)
    lax.fori_loop(0, U - 1, score_and_relay, 0)
    score_chunk(U - 1, 0)

    own(2).wait()

    def take_v(s, c):
        across_in(2, s).wait_recv()
        return c

    lax.fori_loop(0, U, take_v, 0)

    for h in range(heavies):
        def blend(g, acc, h=h):
            rows = V[pl.ds(g * group, group)].reshape(group * TILE, head)
            return acc + jnp.dot(dense_p[h, g], rows, preferred_element_type=jnp.float32)

        acc = lax.fori_loop(0, tiles // group, blend, jnp.zeros((TILE, head), jnp.float32))
        dense_o[h] = acc / dense_o[h]

    def back(s):
        return pltpu.make_async_remote_copy(
            src_ref=o_send.at[s], dst_ref=out.at[u],
            send_sem=osend_sem.at[s], recv_sem=orecv_sem.at[u],
            device_id={"uly": s, "blk": b}, device_id_type=MESH,
        )

    def back_in(s):
        return pltpu.make_async_remote_copy(
            src_ref=o_send.at[s], dst_ref=out.at[s],
            send_sem=osend_sem.at[s], recv_sem=orecv_sem.at[s],
            device_id={"uly": s, "blk": b}, device_id_type=MESH,
        )

    def finish(s):
        for i in range(per):
            tile = (s * 2 + b) * per + i
            slot = s * per + i
            rows = jnp.concatenate([V[pat[0, tile, j]] for j in range(listed)], axis=0)
            res = jnp.dot(probs[slot], rows, preferred_element_type=jnp.float32) / total[slot]
            for h in range(heavies):
                res = jnp.where(heavy[0, h] == tile, dense_o[h], res)
            o_send[s, i] = res.astype(jnp.bfloat16)

    def finish_chunk(c, carry):
        s = flip(u, U - 1 - c, U)
        finish(s)
        back(s).start()
        return carry

    lax.fori_loop(0, U - 1, finish_chunk, 0)
    finish(u)
    mine = pltpu.make_async_copy(o_send.at[u], out.at[u], loc_sem.at[3])
    mine.start()
    mine.wait()

    def close(i, c):
        s = flip(u, i + 1, U)
        for n in range(3):
            away(n, s).wait_send()
            across(n, s).wait_send()
        back(s).wait_send()
        back_in(s).wait_recv()
        return c

    lax.fori_loop(0, U - 1, close, 0)
    for n in range(3):
        own_across(n).wait_send()


def per_device(queries, keys, values, pattern, heavy):
    tokens, heads, head = queries.shape
    U = lax.axis_size("uly")
    per = tokens // TILE
    tiles = U * 2 * per
    group = math.gcd(tiles, 8)
    listed, heavies = pattern.shape[2], heavy.shape[1]

    def by_head(x):
        return x.transpose(1, 0, 2).reshape(heads, per, TILE, head)

    bf = jnp.bfloat16
    any_ = pl.BlockSpec(memory_space=pl.ANY)
    smem = pl.BlockSpec(memory_space=pltpu.SMEM)
    dma = pltpu.SemaphoreType.DMA
    done = pl.pallas_call(
        functools.partial(kernel, U, per),
        out_shape=jax.ShapeDtypeStruct((heads, per, TILE, head), bf),
        in_specs=[smem, smem, any_, any_, any_],
        out_specs=any_,
        scratch_shapes=[
            pltpu.VMEM((tiles, TILE, head), bf),
            pltpu.VMEM((tiles, TILE, head), bf),
            pltpu.VMEM((tiles, TILE, head), bf),
            pltpu.VMEM((tiles // 2, TILE, listed * TILE), bf),
            pltpu.VMEM((tiles // 2, TILE, head), jnp.float32),
            pltpu.VMEM((heavies, tiles // group, TILE, group * TILE), bf),
            pltpu.VMEM((heavies, TILE, head), jnp.float32),
            pltpu.VMEM((U, per, TILE, head), bf),
            dma((3, U)), dma((3, U)), dma((3, U)), dma((3, U)), dma((4,)), dma((U,)), dma((U,)),
        ],
        compiler_params=pltpu.CompilerParams(
            collective_id=0, has_side_effects=True, vmem_limit_bytes=56 * 2 ** 20
        ),
    )(pattern, heavy, by_head(queries), by_head(keys), by_head(values))
    return done.reshape(heads, tokens, head).transpose(1, 0, 2)


def solution(mesh):
    rows = P(("grp", "uly", "blk"), None, None)
    placed = (rows, rows, rows, P(("grp", "uly"), None, None), P(("grp", "uly"), None))
    return jax.shard_map(
        per_device, mesh=mesh, in_specs=placed, out_specs=rows, check_vma=False,
    )
```

time: 128 us -> 70.6 us (0.55)
  Pallas kernels: 0 us -> 62.7 us
  waiting for transfers between devices: 40.3 us -> 0 us
  local copies, waits for them, and re-layouts: 27.7 us -> 7.56 us
  blocking collectives: 18.5 us -> 0 us
  matrix products: 17.8 us -> 0 us
  starting transfers between devices: 16.2 us -> 0 us
  other arithmetic: 5.95 us -> 0 us
    pallas_call x0 -> x1, Pallas kernels: none -> 62.7 us  [per_device(): pl.pallas_call(functools.partial(kernel, U, per), out_shape=jax.ShapeDtyp...]
    all_to_all x3 -> x0, waiting for transfers between devices: 40.3 us -> none  [the longest x1 13.8 us: per_device(): lax.all_to_all(values, 'uly', split_axis=1, concat_axis=0, tiled=True)]
    all_to_all x1 -> x0, blocking collectives: 18.5 us -> none  [per_device(): lax.all_to_all(local_out, 'uly', split_axis=0, concat_axis=1, tiled=True)]
    dot_general x10 -> x0, matrix products: 17.8 us -> none  [the longest x5 10.4 us: attend(): jnp.einsum('gqk,gkd->gqd', probabilities, value_rows, preferred_element_t...]
    gather x10 -> x0, local copies, waits for them, and re-layouts: 16.7 us -> none  [the longest x4 7.89 us: sparse_group(): key_tiles[index_group].reshape(group, listed * TILE, head_size)]
    all_to_all x3 -> x0, starting transfers between devices: 15.1 us -> none  [the longest x1 7.28 us: per_device(): lax.all_to_all(keys, 'uly', split_axis=1, concat_axis=0, tiled=True)]
    transpose x0 -> x3, local copies, waits for them, and re-layouts: none -> 3.72 us  [by_head(): return x.transpose(1, 0, 2).reshape(heads, per, TILE, head)]
    another operation x3 -> x0, other arithmetic: 3.2 us -> none  [the longest x1 2.04 us: per_device(): local_out = jnp.stack(outputs, axis=1)]
  transfers between devices with their start and end apart: 7 -> 0, of which waited for: 3 -> 0; matrix products, arithmetic and copies ran while one was open for 30% -> 0% of each run, Pallas kernels for 0% -> 0%
where the time goes in v1:
time: 70.6 us; the launch traced here: 70.2 us
  Pallas kernels  62.7 us (89%)
  local copies, waits for them, and re-layouts  7.56 us (11%)
    pallas_call x1, Pallas kernels, per_device(): pl.pallas_call(functools.partial(kernel, U, per), out_shape=jax.ShapeDtyp...  62.7 us
    transpose x3, local copies, waits for them, and re-layouts, by_head(): return x.transpose(1, 0, 2).reshape(heads, per, TILE, head)  3.72 us
    reshape x1, local copies, waits for them, and re-layouts, per_device(): return done.reshape(heads, tokens, head).transpose(1, 0, 2)  2.18 us
    unnamed x7, local copies, waits for them, and re-layouts  1.67 us

profile of v1, /device:TPU:0, one launch (start us, length us, event | category | flops | bytes accessed | tf_op | source)
XLA Modules:
  0.0 70.2 jit_solution(13452751101559008496)
XLA Ops:
  0.0 0.0 copy-start.2
  0.0 0.7 copy-done.2
  0.7 0.7 copy.9.pat
  1.4 0.0 copy-start
  1.4 2.0 %copy.6 = bf16[8,256,128]{2,1,0:T(8,128)(2,1)} copy(bf16[8,256,128]{2,0,1:T(8,128)(2,1)} %bitcast.14) | data formatting | bytes 1048576 | tf_op jit(solution)/shard_map/transpose | solution.py:247
  3.3 0.0 copy-done
  3.3 0.0 copy-start.1
  3.3 0.9 %copy.7 = bf16[8,256,128]{2,1,0:T(8,128)(2,1)} copy(bf16[8,256,128]{2,0,1:T(8,128)(2,1)S(1)} %bitcast.15) | data formatting | bytes 1048576 | tf_op jit(solution)/shard_map/transpose | solution.py:247
  4.2 0.3 copy-done.1
  4.5 0.9 %copy.8 = bf16[8,256,128]{2,1,0:T(8,128)(2,1)} copy(bf16[8,256,128]{2,0,1:T(8,128)(2,1)S(1)} %bitcast.16) | data formatting | bytes 1048576 | tf_op jit(solution)/shard_map/transpose | solution.py:247
  5.4 62.7 %shard_map.55 = bf16[8,2,128,128]{3,2,1,0:T(8,128)(2,1)} custom-call(s32[1,32,8]{2,1,0:T(8,128)} %copy.9.pat, s32[1,2]{1,0:T(1,128)} %heavy.1, bf16[8,2,128,128]{3,2,1,0:T(8,128)(2,1)} %bitcast.11, bf16[8,2,128,128]{3,2,1,0:T(8,128)(2,1)} %bitcast.12, bf16[8,2,128,128]{3,2,1,0:T(8,128)(2,1)} %bitcast.13), custom_call_target="tpu_custom_call" | custom-call | tf_op jit(solution)/shard_map/pallas_call | solution.py:253
  68.1 2.2 %copy.12 = bf16[8,256,128]{2,0,1:T(8,128)(2,1)} copy(bf16[8,256,128]{2,1,0:T(8,128)(2,1)} %bitcast.10) | data formatting | bytes 1048576 | tf_op jit(solution)/shard_map/reshape | solution.py:273
Async XLA Ops:
  0.0 0.7 copy-start.2
  1.4 2.0 %copy-start = (bf16[256,8,128]{2,1,0:T(8,128)(2,1)S(1)}, bf16[256,8,128]{2,1,0:T(8,128)(2,1)}, u32[]{:S(2)}) copy-start(bf16[256,8,128]{2,1,0:T(8,128)(2,1)} %param.6) | copy-start | bytes 1572868
  3.3 1.2 %copy-start.1 = (bf16[256,8,128]{2,1,0:T(8,128)(2,1)S(1)}, bf16[256,8,128]{2,1,0:T(8,128)(2,1)}, u32[]{:S(2)}) copy-start(bf16[256,8,128]{2,1,0:T(8,128)(2,1)} %param.7) | copy-start | bytes 1572868

commit v2 on v1

--- a/solution.py
+++ b/solution.py
@@ -23,17 +23,18 @@
 
 
 def kernel(
-    U, per, pat, heavy, q_in, k_in, v_in, out,
-    Q, K, V, probs, total, dense_p, dense_o, o_send,
-    send_sem, recv_sem, fsend_sem, frecv_sem, loc_sem, osend_sem, orecv_sem,
+    U, per, pat_in, heavy_in, q_in, k_in, v_in, out,
+    Q, K, V, probs, total, dense_p, dense_o, o_send, pat, heavy, staged, wide, k_s, q_s, v_s,
+    send_sem, recv_sem, fsend_sem, frecv_sem, loc_sem, osend_sem, orecv_sem, in_sem,
 ):
     u, b = lax.axis_index("uly"), lax.axis_index("blk")
     sib = 1 - b
     tiles, head = K.shape[0], K.shape[2]
     listed, heavies = pat.shape[2], heavy.shape[1]
     c2 = head ** (-0.5) * math.log2(math.e)
-    group = math.gcd(tiles, 8)
-    bufs, ins = (K, Q, V), (k_in, q_in, v_in)
+    group = 2 * per
+    bufs, ins = (K, Q, V), (k_s, q_s, v_s)
+    heads = staged.shape[2]
 
     barrier = pltpu.get_barrier_semaphore()
 
@@ -45,6 +46,35 @@
 
     lax.fori_loop(1, U, greet, 0)
     pl.semaphore_signal(barrier, inc=1, device_id={"uly": u, "blk": sib}, device_id_type=MESH)
+
+    def fetch(n):
+        return pltpu.make_async_copy((k_in, q_in, v_in)[n], staged.at[n], in_sem.at[n])
+
+    tables = (
+        pltpu.make_async_copy(pat_in, pat, in_sem.at[3]),
+        pltpu.make_async_copy(heavy_in, heavy, in_sem.at[4]),
+    )
+    for n in range(3):
+        fetch(n).start()
+    for copy in tables:
+        copy.start()
+
+    def widen(n):
+        fetch(n).wait()
+        for r in range(per):
+            rows = staged[n, r * TILE:(r + 1) * TILE].astype(jnp.float32)
+            wide[r] = rows.reshape(TILE * heads, head)
+
+    def split(n, s):
+        for r in range(per):
+            ins[n][s, r] = wide[r, pl.ds(s, TILE, stride=heads), :].astype(jnp.bfloat16)
+
+    def split_all(s, c):
+        split(0, s)
+        return c
+
+    widen(0)
+    lax.fori_loop(0, U, split_all, 0)
     pl.semaphore_wait(barrier, U)
 
     def at(buf, s, half):
@@ -90,10 +120,17 @@
 
     for n in range(3):
         def push(i, c, n=n):
-            away(n, flip(u, U - 1 - i, U)).start()
+            s = flip(u, U - 1 - i, U)
+            if n:
+                split(n, s)
+            away(n, s).start()
             return c
 
+        if n:
+            widen(n)
         lax.fori_loop(0, U - 1, push, 0)
+        if n:
+            split(n, u)
         own(n).start()
         own_across(n).start()
 
@@ -101,20 +138,21 @@
         arriving(n, s).wait_recv()
         across(n, s).start()
 
-    for n in range(2):
-        def pass_on(i, c, n=n):
-            relay(n, flip(u, U - 1 - i, U))
-            return c
-
-        lax.fori_loop(0, U - 1, pass_on, 0)
-    for n in range(2):
-        own(n).wait()
-
-        def take(s, c, n=n):
-            across_in(n, s).wait_recv()
-            return c
-
-        lax.fori_loop(0, U, take, 0)
+    def pass_on(i, c):
+        relay(0, flip(u, U - 1 - i, U))
+        return c
+
+    lax.fori_loop(0, U - 1, pass_on, 0)
+    own(0).wait()
+    own(1).wait()
+    for copy in tables:
+        copy.wait()
+
+    def take(s, c, n=0):
+        across_in(n, s).wait_recv()
+        return c
+
+    lax.fori_loop(0, U, take, 0)
 
     def scores(query, key_rows):
         return lax.dot_general(
@@ -138,10 +176,9 @@
 
         return carry
 
-    def score_and_relay(c, carry):
-        score_chunk(c, carry)
-        relay(2, flip(u, U - 1 - c, U))
-        return carry
+    def relay_and_score(c, carry):
+        relay(1, flip(u, U - 1 - c, U))
+        return score_chunk(c, carry)
 
     def dense_scores(h):
         query = Q[heavy[0, h]]
@@ -164,25 +201,32 @@
         acc = lax.fori_loop(0, tiles // group, weigh, jnp.zeros((TILE, 1), jnp.float32))
         dense_o[h] = jnp.broadcast_to(acc, (TILE, head))
 
+    score_chunk(U - 1, 0)
+    lax.fori_loop(0, U - 1, relay_and_score, 0)
+    lax.fori_loop(0, U, functools.partial(take, n=1), 0)
     for h in range(heavies):
         dense_scores(h)
-    lax.fori_loop(0, U - 1, score_and_relay, 0)
-    score_chunk(U - 1, 0)
-
     own(2).wait()
 
-    def take_v(s, c):
-        across_in(2, s).wait_recv()
-        return c
-
-    lax.fori_loop(0, U, take_v, 0)
-
-    for h in range(heavies):
-        def blend(g, acc, h=h):
-            rows = V[pl.ds(g * group, group)].reshape(group * TILE, head)
-            return acc + jnp.dot(dense_p[h, g], rows, preferred_element_type=jnp.float32)
-
-        acc = lax.fori_loop(0, tiles // group, blend, jnp.zeros((TILE, head), jnp.float32))
+    def blend(s, accs):
+        rows = V[pl.ds(s * 2 * per, 2 * per)].reshape(2 * per * TILE, head)
+        return tuple(
+            acc + jnp.dot(dense_p[h, s], rows, preferred_element_type=jnp.float32)
+            for h, acc in enumerate(accs)
+        )
+
+    def relay_and_blend(c, accs):
+        s = flip(u, U - 1 - c, U)
+        relay(2, s)
+        before = jnp.where(c == 0, u, flip(u, U - c, U))
+        across_in(2, before).wait_recv()
+        return blend(before, accs)
+
+    accs = tuple(jnp.zeros((TILE, head), jnp.float32) for _ in range(heavies))
+    accs = lax.fori_loop(0, U - 1, relay_and_blend, accs)
+    last = flip(u, 1, U)
+    across_in(2, last).wait_recv()
+    for h, acc in enumerate(blend(last, accs)):
         dense_o[h] = acc / dense_o[h]
 
     def back(s):
@@ -240,20 +284,17 @@
     U = lax.axis_size("uly")
     per = tokens // TILE
     tiles = U * 2 * per
-    group = math.gcd(tiles, 8)
+    group = 2 * per
     listed, heavies = pattern.shape[2], heavy.shape[1]
 
-    def by_head(x):
-        return x.transpose(1, 0, 2).reshape(heads, per, TILE, head)
 
     bf = jnp.bfloat16
     any_ = pl.BlockSpec(memory_space=pl.ANY)
-    smem = pl.BlockSpec(memory_space=pltpu.SMEM)
     dma = pltpu.SemaphoreType.DMA
     done = pl.pallas_call(
         functools.partial(kernel, U, per),
         out_shape=jax.ShapeDtypeStruct((heads, per, TILE, head), bf),
-        in_specs=[smem, smem, any_, any_, any_],
+        in_specs=[any_] * 5,
         out_specs=any_,
         scratch_shapes=[
             pltpu.VMEM((tiles, TILE, head), bf),
@@ -264,12 +305,17 @@
             pltpu.VMEM((heavies, tiles // group, TILE, group * TILE), bf),
             pltpu.VMEM((heavies, TILE, head), jnp.float32),
             pltpu.VMEM((U, per, TILE, head), bf),
-            dma((3, U)), dma((3, U)), dma((3, U)), dma((3, U)), dma((4,)), dma((U,)), dma((U,)),
+            pltpu.SMEM(pattern.shape, jnp.int32),
+            pltpu.SMEM(heavy.shape, jnp.int32),
+            pltpu.VMEM((3, tokens, heads, head), bf),
+            pltpu.VMEM((per, TILE * heads, head), jnp.float32),
+            *[pltpu.VMEM((U, per, TILE, head), bf)] * 3,
+            dma((3, U)), dma((3, U)), dma((3, U)), dma((3, U)), dma((4,)), dma((U,)), dma((U,)), dma((5,)),
         ],
         compiler_params=pltpu.CompilerParams(
-            collective_id=0, has_side_effects=True, vmem_limit_bytes=56 * 2 ** 20
+            collective_id=0, has_side_effects=True, vmem_limit_bytes=60 * 2 ** 20
         ),
-    )(pattern, heavy, by_head(queries), by_head(keys), by_head(values))
+    )(pattern, heavy, queries, keys, values)
     return done.reshape(heads, tokens, head).transpose(1, 0, 2)
 
 

time: 70.6 us -> 69.8 us (0.989)
  local copies, waits for them, and re-layouts: 7.56 us -> 3.54 us
  Pallas kernels: 62.7 us -> 66 us
    transpose x3 -> x0, local copies, waits for them, and re-layouts: 3.72 us -> none  [by_head(): return x.transpose(1, 0, 2).reshape(heads, per, TILE, head)]
    pallas_call x1, Pallas kernels: 62.7 us -> 66 us  [per_device(): pl.pallas_call(functools.partial(kernel, U, per), out_shape=jax.ShapeDtyp...]
    unnamed x7 -> x1, local copies, waits for them, and re-layouts: 1.67 us -> 1.37 us
where the time goes in v2:
time: 69.8 us; the launch traced here: 69.6 us
  Pallas kernels  66 us (95%)
  local copies, waits for them, and re-layouts  3.54 us (5%)
    pallas_call x1, Pallas kernels, per_device(): pl.pallas_call(functools.partial(kernel, U, per), out_shape=jax.ShapeDtyp...  66 us
    reshape x1, local copies, waits for them, and re-layouts, per_device(): return done.reshape(heads, tokens, head).transpose(1, 0, 2)  2.18 us

profile of v2, /device:TPU:0, one launch (start us, length us, event | category | flops | bytes accessed | tf_op | source)
XLA Modules:
  0.0 69.6 jit_solution(2795474734805323792)
XLA Ops:
  0.0 1.4 %copy.6.pat_in = s32[1,32,8]{2,1,0:T(8,128)} copy(s32[1,32,8]{1,2,0:T(8,128)} %param.8) | data formatting | bytes 2048 | tf_op args[3]
  1.4 66.0 %shard_map.55 = bf16[8,2,128,128]{3,2,1,0:T(8,128)(2,1)} custom-call(s32[1,32,8]{2,1,0:T(8,128)} %copy.6.pat_in, s32[1,2]{1,0:T(1,128)} %heavy_in.1, bf16[256,8,128]{2,1,0:T(8,128)(2,1)} %q_in.1, bf16[256,8,128]{2,1,0:T(8,128)(2,1)} %k_in.1, bf16[256,8,128]{2,1,0:T(8,128)(2,1)} %v_in.1), custom_call_target="tpu_custom_call" | custom-call | tf_op jit(solution)/shard_map/pallas_call | solution.py:294
  67.4 2.2 %copy.9 = bf16[8,256,128]{2,0,1:T(8,128)(2,1)} copy(bf16[8,256,128]{2,1,0:T(8,128)(2,1)} %bitcast.4) | data formatting | bytes 1048576 | tf_op jit(solution)/shard_map/reshape | solution.py:319

commit v3 on v2

--- a/solution.py
+++ b/solution.py
@@ -164,9 +164,9 @@
         slot = s * per + i
         rows = jnp.concatenate([K[pat[0, tile, j]] for j in range(listed)], axis=0)
         sc = scores(Q[tile], rows)
-        top = jnp.max(sc, axis=-1, keepdims=True)
+        top = jnp.max(fold(jnp.maximum, sc), axis=-1, keepdims=True)
         w = jnp.exp2((sc - top) * c2)
-        total[slot] = jnp.broadcast_to(jnp.sum(w, axis=-1, keepdims=True), (TILE, head))
+        total[slot] = jnp.broadcast_to(jnp.sum(fold(jnp.add, w), axis=-1, keepdims=True), (TILE, head))
         probs[slot] = w.astype(jnp.bfloat16)
 
     def score_chunk(c, carry):
@@ -180,32 +180,54 @@
         relay(1, flip(u, U - 1 - c, U))
         return score_chunk(c, carry)
 
-    def dense_scores(h):
-        query = Q[heavy[0, h]]
+    def fold(op, x):
+        parts = [x[:, k * head:(k + 1) * head] for k in range(x.shape[1] // head)]
+        while len(parts) > 1:
+            parts = [op(*parts[k:k + 2]) if k + 1 < len(parts) else parts[k]
+                     for k in range(0, len(parts), 2)]
+        return parts[0]
+
+    def dense_scores():
+        steps = tiles // group
+        asked = [Q[heavy[0, h]] for h in range(heavies)]
 
         def keys_of(g):
             return K[pl.ds(g * group, group)].reshape(group * TILE, head)
 
-        def top_of(g, top):
-            return jnp.maximum(top, jnp.max(scores(query, keys_of(g)), axis=-1, keepdims=True))
-
-        top = lax.fori_loop(
-            0, tiles // group, top_of, jnp.full((TILE, 1), -jnp.inf, jnp.float32)
-        )
-
-        def weigh(g, acc):
-            w = jnp.exp2((scores(query, keys_of(g)) - top) * c2)
-            dense_p[h, g] = w.astype(jnp.bfloat16)
-            return acc + jnp.sum(w, axis=-1, keepdims=True)
-
-        acc = lax.fori_loop(0, tiles // group, weigh, jnp.zeros((TILE, 1), jnp.float32))
-        dense_o[h] = jnp.broadcast_to(acc, (TILE, head))
+        def top_of(g, tops):
+            rows = keys_of(g)
+            return tuple(
+                jnp.maximum(top, fold(jnp.maximum, scores(query, rows)))
+                for query, top in zip(asked, tops)
+            )
+
+        tops = lax.fori_loop(
+            0, steps, top_of, (jnp.full((TILE, head), -jnp.inf, jnp.float32),) * heavies,
+            unroll=math.gcd(steps, 4),
+        )
+        tops = [jnp.max(top, axis=-1, keepdims=True) for top in tops]
+
+        def weigh(g, accs):
+            rows, new = keys_of(g), []
+            for h in range(heavies):
+                w = jnp.exp2((scores(asked[h], rows) - tops[h]) * c2)
+                dense_p[h, g] = w.astype(jnp.bfloat16)
+                new.append(accs[h] + fold(jnp.add, w))
+            return tuple(new)
+
+        accs = lax.fori_loop(
+            0, steps, weigh, (jnp.zeros((TILE, head), jnp.float32),) * heavies,
+            unroll=math.gcd(steps, 4),
+        )
+        for h in range(heavies):
+            dense_o[h] = jnp.broadcast_to(
+                jnp.sum(accs[h], axis=-1, keepdims=True), (TILE, head)
+            )
 
     score_chunk(U - 1, 0)
     lax.fori_loop(0, U - 1, relay_and_score, 0)
     lax.fori_loop(0, U, functools.partial(take, n=1), 0)
-    for h in range(heavies):
-        dense_scores(h)
+    dense_scores()
     own(2).wait()
 
     def blend(s, accs):

time: 69.8 us -> 63 us (0.903)
  Pallas kernels: 66 us -> 59.2 us
    pallas_call x1, Pallas kernels: 66 us -> 59.2 us  [per_device(): pl.pallas_call(functools.partial(kernel, U, per), out_shape=jax.ShapeDtyp...]
where the time goes in v3:
time: 63 us; the launch traced here: 62.8 us
  Pallas kernels  59.2 us (94%)
  local copies, waits for them, and re-layouts  3.54 us (6%)
    pallas_call x1, Pallas kernels, per_device(): pl.pallas_call(functools.partial(kernel, U, per), out_shape=jax.ShapeDtyp...  59.2 us
    reshape x1, local copies, waits for them, and re-layouts, per_device(): return done.reshape(heads, tokens, head).transpose(1, 0, 2)  2.18 us
    unnamed x1, local copies, waits for them, and re-layouts  1.37 us

profile of v3, /device:TPU:0, one launch (start us, length us, event | category | flops | bytes accessed | tf_op | source)
XLA Modules:
  0.0 62.8 jit_solution(4383744853674671981)
XLA Ops:
  0.0 1.4 %copy.6.pat_in = s32[1,32,8]{2,1,0:T(8,128)} copy(s32[1,32,8]{1,2,0:T(8,128)} %param.8) | data formatting | bytes 2048 | tf_op args[3]
  1.4 59.2 %shard_map.55 = bf16[8,2,128,128]{3,2,1,0:T(8,128)(2,1)} custom-call(s32[1,32,8]{2,1,0:T(8,128)} %copy.6.pat_in, s32[1,2]{1,0:T(1,128)} %heavy_in.1, bf16[256,8,128]{2,1,0:T(8,128)(2,1)} %q_in.1, bf16[256,8,128]{2,1,0:T(8,128)(2,1)} %k_in.1, bf16[256,8,128]{2,1,0:T(8,128)(2,1)} %v_in.1), custom_call_target="tpu_custom_call" | custom-call | tf_op jit(solution)/shard_map/pallas_call | solution.py:316
  60.6 2.2 %copy.9 = bf16[8,256,128]{2,0,1:T(8,128)(2,1)} copy(bf16[8,256,128]{2,1,0:T(8,128)(2,1)} %bitcast.4) | data formatting | bytes 1048576 | tf_op jit(solution)/shard_map/reshape | solution.py:341

commit v4 on v3

--- a/solution.py
+++ b/solution.py
@@ -24,17 +24,18 @@
 
 def kernel(
     U, per, pat_in, heavy_in, q_in, k_in, v_in, out,
-    Q, K, V, probs, total, dense_p, dense_o, o_send, pat, heavy, staged, wide, k_s, q_s, v_s,
+    Q, K, V, probs, total, dense_p, dense_o, pat, heavy, staged, wide, k_s, q_s, v_s, o_got,
     send_sem, recv_sem, fsend_sem, frecv_sem, loc_sem, osend_sem, orecv_sem, in_sem,
 ):
     u, b = lax.axis_index("uly"), lax.axis_index("blk")
     sib = 1 - b
     tiles, head = K.shape[0], K.shape[2]
-    listed, heavies = pat.shape[2], heavy.shape[1]
+    listed, heavies = pat.shape[1], heavy.shape[1]
     c2 = head ** (-0.5) * math.log2(math.e)
     group = 2 * per
     bufs, ins = (K, Q, V), (k_s, q_s, v_s)
     heads = staged.shape[2]
+    o_send = k_s
 
     barrier = pltpu.get_barrier_semaphore()
 
@@ -162,7 +163,7 @@
     def score_tile(s, i):
         tile = (s * 2 + b) * per + i
         slot = s * per + i
-        rows = jnp.concatenate([K[pat[0, tile, j]] for j in range(listed)], axis=0)
+        rows = jnp.concatenate([K[pat[0, j, tile]] for j in range(listed)], axis=0)
         sc = scores(Q[tile], rows)
         top = jnp.max(fold(jnp.maximum, sc), axis=-1, keepdims=True)
         w = jnp.exp2((sc - top) * c2)
@@ -224,6 +225,13 @@
                 jnp.sum(accs[h], axis=-1, keepdims=True), (TILE, head)
             )
 
+    def sent_keys(i, c):
+        s = flip(u, i + 1, U)
+        away(0, s).wait_send()
+        return c
+
+    lax.fori_loop(0, U - 1, sent_keys, 0)
+    own_across(0).wait_send()
     score_chunk(U - 1, 0)
     lax.fori_loop(0, U - 1, relay_and_score, 0)
     lax.fori_loop(0, U, functools.partial(take, n=1), 0)
@@ -253,14 +261,14 @@
 
     def back(s):
         return pltpu.make_async_remote_copy(
-            src_ref=o_send.at[s], dst_ref=out.at[u],
+            src_ref=o_send.at[s], dst_ref=o_got.at[u],
             send_sem=osend_sem.at[s], recv_sem=orecv_sem.at[u],
             device_id={"uly": s, "blk": b}, device_id_type=MESH,
         )
 
     def back_in(s):
         return pltpu.make_async_remote_copy(
-            src_ref=o_send.at[s], dst_ref=out.at[s],
+            src_ref=o_send.at[s], dst_ref=o_got.at[s],
             send_sem=osend_sem.at[s], recv_sem=orecv_sem.at[s],
             device_id={"uly": s, "blk": b}, device_id_type=MESH,
         )
@@ -269,7 +277,7 @@
         for i in range(per):
             tile = (s * 2 + b) * per + i
             slot = s * per + i
-            rows = jnp.concatenate([V[pat[0, tile, j]] for j in range(listed)], axis=0)
+            rows = jnp.concatenate([V[pat[0, j, tile]] for j in range(listed)], axis=0)
             res = jnp.dot(probs[slot], rows, preferred_element_type=jnp.float32) / total[slot]
             for h in range(heavies):
                 res = jnp.where(heavy[0, h] == tile, dense_o[h], res)
@@ -283,22 +291,39 @@
 
     lax.fori_loop(0, U - 1, finish_chunk, 0)
     finish(u)
-    mine = pltpu.make_async_copy(o_send.at[u], out.at[u], loc_sem.at[3])
-    mine.start()
-    mine.wait()
+
+    def place(buf, s):
+        for r in range(per):
+            wide[r, pl.ds(s, TILE, stride=heads), :] = buf[s, r].astype(jnp.float32)
+
+    place(o_send, u)
+
+    def land(i, c):
+        s = flip(u, U - 1 - i, U)
+        back_in(s).wait_recv()
+        place(o_got, s)
+        return c
+
+    lax.fori_loop(0, U - 1, land, 0)
+    for r in range(per):
+        rows = wide[r].reshape(TILE, heads, head)
+        staged[0, r * TILE:(r + 1) * TILE] = rows.astype(jnp.bfloat16)
+    written = pltpu.make_async_copy(staged.at[0], out, loc_sem.at[3])
+    written.start()
 
     def close(i, c):
         s = flip(u, i + 1, U)
         for n in range(3):
-            away(n, s).wait_send()
+            if n:
+                away(n, s).wait_send()
             across(n, s).wait_send()
         back(s).wait_send()
-        back_in(s).wait_recv()
         return c
 
     lax.fori_loop(0, U - 1, close, 0)
-    for n in range(3):
+    for n in range(1, 3):
         own_across(n).wait_send()
+    written.wait()
 
 
 def per_device(queries, keys, values, pattern, heavy):
@@ -313,9 +338,9 @@
     bf = jnp.bfloat16
     any_ = pl.BlockSpec(memory_space=pl.ANY)
     dma = pltpu.SemaphoreType.DMA
-    done = pl.pallas_call(
+    return pl.pallas_call(
         functools.partial(kernel, U, per),
-        out_shape=jax.ShapeDtypeStruct((heads, per, TILE, head), bf),
+        out_shape=jax.ShapeDtypeStruct((tokens, heads, head), bf),
         in_specs=[any_] * 5,
         out_specs=any_,
         scratch_shapes=[
@@ -326,19 +351,17 @@
             pltpu.VMEM((tiles // 2, TILE, head), jnp.float32),
             pltpu.VMEM((heavies, tiles // group, TILE, group * TILE), bf),
             pltpu.VMEM((heavies, TILE, head), jnp.float32),
-            pltpu.VMEM((U, per, TILE, head), bf),
-            pltpu.SMEM(pattern.shape, jnp.int32),
+            pltpu.SMEM((1, listed, tiles), jnp.int32),
             pltpu.SMEM(heavy.shape, jnp.int32),
             pltpu.VMEM((3, tokens, heads, head), bf),
             pltpu.VMEM((per, TILE * heads, head), jnp.float32),
-            *[pltpu.VMEM((U, per, TILE, head), bf)] * 3,
+            *[pltpu.VMEM((U, per, TILE, head), bf)] * 4,
             dma((3, U)), dma((3, U)), dma((3, U)), dma((3, U)), dma((4,)), dma((U,)), dma((U,)), dma((5,)),
         ],
         compiler_params=pltpu.CompilerParams(
             collective_id=0, has_side_effects=True, vmem_limit_bytes=60 * 2 ** 20
         ),
-    )(pattern, heavy, queries, keys, values)
-    return done.reshape(heads, tokens, head).transpose(1, 0, 2)
+    )(pattern.transpose(0, 2, 1), heavy, queries, keys, values)
 
 
 def solution(mesh):

time: 63 us -> 62.1 us (0.986)
  local copies, waits for them, and re-layouts: 3.54 us -> 1.87 us
  Pallas kernels: 59.2 us -> 60.1 us
    reshape x1 -> x0, local copies, waits for them, and re-layouts: 2.18 us -> none  [per_device(): return done.reshape(heads, tokens, head).transpose(1, 0, 2)]
    pallas_call x1, Pallas kernels: 59.2 us -> 60.1 us  [per_device(): pl.pallas_call(functools.partial(kernel, U, per), out_shape=jax.ShapeDtyp...]
where the time goes in v4:
time: 62.1 us; the launch traced here: 62 us
  Pallas kernels  60.1 us (97%)
  local copies, waits for them, and re-layouts  1.87 us (3%)
    pallas_call x1, Pallas kernels, per_device(): pl.pallas_call(functools.partial(kernel, U, per), out_shape=jax.ShapeDtyp...  60.1 us
    unnamed x1, local copies, waits for them, and re-layouts  1.87 us

profile of v4, /device:TPU:0, one launch (start us, length us, event | category | flops | bytes accessed | tf_op | source)
XLA Modules:
  0.0 62.0 jit_solution(17319171911343303724)
XLA Ops:
  0.0 60.1 %shard_map.55 = bf16[256,8,128]{2,1,0:T(8,128)(2,1)} custom-call(s32[1,8,32]{2,1,0:T(8,128)} %bitcast.1, s32[1,2]{1,0:T(1,128)} %heavy_in.1, bf16[256,8,128]{2,1,0:T(8,128)(2,1)} %q_in.1, bf16[256,8,128]{2,1,0:T(8,128)(2,1)} %k_in.1, bf16[256,8,128]{2,1,0:T(8,128)(2,1)} %v_in.1), custom_call_target="tpu_custom_call" | custom-call | tf_op jit(solution)/shard_map/pallas_call | solution.py:341
  60.1 1.9 %copy.7 = bf16[256,8,128]{2,1,0:T(8,128)(2,1)} copy(bf16[256,8,128]{2,1,0:T(8,128)(2,1)} %shard_map.55) | data formatting | bytes 1048576

commit v5 on v4

--- a/solution.py
+++ b/solution.py
@@ -119,21 +119,31 @@
             device_id={"uly": u, "blk": sib}, device_id_type=MESH,
         )
 
+    def early(s):
+        return (s % 2 + s // 2 % 2) % 2 == 0
+
+    def push(i, c, n, first):
+        s = flip(u, U - 1 - i, U)
+
+        @pl.when(early(s) == first)
+        def _():
+            away(n, s).start()
+
+        return c
+
+    def split_one(s, c, n):
+        split(n, s)
+        return c
+
     for n in range(3):
-        def push(i, c, n=n):
-            s = flip(u, U - 1 - i, U)
-            if n:
-                split(n, s)
-            away(n, s).start()
-            return c
-
         if n:
             widen(n)
-        lax.fori_loop(0, U - 1, push, 0)
-        if n:
-            split(n, u)
+            lax.fori_loop(0, U, functools.partial(split_one, n=n), 0)
+        lax.fori_loop(0, U - 1, functools.partial(push, n=n, first=True), 0)
         own(n).start()
         own_across(n).start()
+    for n in range(3):
+        lax.fori_loop(0, U - 1, functools.partial(push, n=n, first=False), 0)
 
     def relay(n, s):
         arriving(n, s).wait_recv()
@@ -289,6 +299,11 @@
         back(s).start()
         return carry
 
+    def sent_rows(i, c):
+        away(2, flip(u, i + 1, U)).wait_send()
+        return c
+
+    lax.fori_loop(0, U - 1, sent_rows, 0)
     lax.fori_loop(0, U - 1, finish_chunk, 0)
     finish(u)
 
@@ -298,13 +313,18 @@
 
     place(o_send, u)
 
-    def land(i, c):
+    def land(i, c, first):
         s = flip(u, U - 1 - i, U)
-        back_in(s).wait_recv()
-        place(o_got, s)
-        return c
-
-    lax.fori_loop(0, U - 1, land, 0)
+
+        @pl.when(early(s) == first)
+        def _():
+            back_in(s).wait_recv()
+            place(o_got, s)
+
+        return c
+
+    for first in (True, False):
+        lax.fori_loop(0, U - 1, functools.partial(land, first=first), 0)
     for r in range(per):
         rows = wide[r].reshape(TILE, heads, head)
         staged[0, r * TILE:(r + 1) * TILE] = rows.astype(jnp.bfloat16)
@@ -314,7 +334,7 @@
     def close(i, c):
         s = flip(u, i + 1, U)
         for n in range(3):
-            if n:
+            if n == 1:
                 away(n, s).wait_send()
             across(n, s).wait_send()
         back(s).wait_send()

time: 62.1 us -> 64 us (1.031)
  Pallas kernels: 60.1 us -> 62 us
    pallas_call x1, Pallas kernels: 60.1 us -> 62 us  [per_device(): pl.pallas_call(functools.partial(kernel, U, per), out_shape=jax.ShapeDtyp...]
where the time goes in v5:
time: 64 us; the launch traced here: 63.9 us
  Pallas kernels  62 us (97%)
  local copies, waits for them, and re-layouts  1.87 us (3%)
    pallas_call x1, Pallas kernels, per_device(): pl.pallas_call(functools.partial(kernel, U, per), out_shape=jax.ShapeDtyp...  62 us
    unnamed x1, local copies, waits for them, and re-layouts  1.87 us

profile of v5, /device:TPU:0, one launch (start us, length us, event | category | flops | bytes accessed | tf_op | source)
XLA Modules:
  0.0 63.9 jit_solution(7364069075350400251)
XLA Ops:
  0.0 62.0 %shard_map.55 = bf16[256,8,128]{2,1,0:T(8,128)(2,1)} custom-call(s32[1,8,32]{2,1,0:T(8,128)} %bitcast.1, s32[1,2]{1,0:T(1,128)} %heavy_in.1, bf16[256,8,128]{2,1,0:T(8,128)(2,1)} %q_in.1, bf16[256,8,128]{2,1,0:T(8,128)(2,1)} %k_in.1, bf16[256,8,128]{2,1,0:T(8,128)(2,1)} %v_in.1), custom_call_target="tpu_custom_call" | custom-call | tf_op jit(solution)/shard_map/pallas_call | solution.py:361
  62.0 1.9 %copy.7 = bf16[256,8,128]{2,1,0:T(8,128)(2,1)} copy(bf16[256,8,128]{2,1,0:T(8,128)(2,1)} %shard_map.55) | data formatting | bytes 1048576

commit v6 on v4

--- a/solution.py
+++ b/solution.py
@@ -359,7 +359,7 @@
             dma((3, U)), dma((3, U)), dma((3, U)), dma((3, U)), dma((4,)), dma((U,)), dma((U,)), dma((5,)),
         ],
         compiler_params=pltpu.CompilerParams(
-            collective_id=0, has_side_effects=True, vmem_limit_bytes=60 * 2 ** 20
+            collective_id=0, has_side_effects=True, vmem_limit_bytes=min(60 * 2 ** 20, (tiles * 15 // 32 + 9) * 2 ** 20)
         ),
     )(pattern.transpose(0, 2, 1), heavy, queries, keys, values)
 

time: 62.1 us -> 65.1 us (1.048)
  local copies, waits for them, and re-layouts: 1.87 us -> 5.26 us
    unnamed x1 -> x11, local copies, waits for them, and re-layouts: 1.87 us -> 5.26 us
where the time goes in v6:
time: 65.1 us; the launch traced here: 64.8 us
  Pallas kernels  59.5 us (91%)
  local copies, waits for them, and re-layouts  5.26 us (8%)
    pallas_call x1, Pallas kernels, per_device(): pl.pallas_call(functools.partial(kernel, U, per), out_shape=jax.ShapeDtyp...  59.5 us
    unnamed x11, local copies, waits for them, and re-layouts  5.26 us

profile of v6, /device:TPU:0, one launch (start us, length us, event | category | flops | bytes accessed | tf_op | source)
XLA Modules:
  0.0 64.8 jit_solution(18351330214009712332)
XLA Ops:
  0.0 0.0 copy-start.4
  0.0 0.7 %copy-done.4 = s32[1,2]{1,0:T(1,128)S(1)} copy-done((s32[1,2]{1,0:T(1,128)S(1)}, s32[1,2]{1,0:T(1,128)}, u32[]{:S(2)}) %copy-start.4) | copy-done | bytes 32
  0.7 0.0 copy-start
  0.7 1.0 %copy-done = bf16[256,8,128]{2,1,0:T(8,128)(2,1)S(1)} copy-done((bf16[256,8,128]{2,1,0:T(8,128)(2,1)S(1)}, bf16[256,8,128]{2,1,0:T(8,128)(2,1)}, u32[]{:S(2)}) %copy-start) | copy-done | bytes 524312
  1.7 0.0 copy-start.1
  1.7 1.0 %copy-done.1 = bf16[256,8,128]{2,1,0:T(8,128)(2,1)S(1)} copy-done((bf16[256,8,128]{2,1,0:T(8,128)(2,1)S(1)}, bf16[256,8,128]{2,1,0:T(8,128)(2,1)}, u32[]{:S(2)}) %copy-start.1) | copy-done | bytes 524312
  2.7 0.0 copy-start.2
  2.7 1.0 %copy-done.2 = bf16[256,8,128]{2,1,0:T(8,128)(2,1)S(1)} copy-done((bf16[256,8,128]{2,1,0:T(8,128)(2,1)S(1)}, bf16[256,8,128]{2,1,0:T(8,128)(2,1)}, u32[]{:S(2)}) %copy-start.2) | copy-done | bytes 524312
  3.8 0.0 copy-start.3
  3.8 0.7 %copy-done.3 = s32[1,32,8]{1,2,0:T(8,128)S(1)} copy-done((s32[1,32,8]{1,2,0:T(8,128)S(1)}, s32[1,32,8]{1,2,0:T(8,128)}, u32[]{:S(2)}) %copy-start.3) | copy-done | bytes 1048
  4.5 59.5 %shard_map.55 = bf16[256,8,128]{2,1,0:T(8,128)(2,1)S(1)} custom-call(s32[1,8,32]{2,1,0:T(8,128)S(1)} %bitcast.1, s32[1,2]{1,0:T(1,128)S(1)} %copy-done.4, bf16[256,8,128]{2,1,0:T(8,128)(2,1)S(1)} %copy-done, bf16[256,8,128]{2,1,0:T(8,128)(2,1)S(1)} %copy-done.1, bf16[256,8,128]{2,1,0:T(8,128)(2,1)S(1)} %copy-done.2), custom_call_target="tpu_custom_call" | custom-call | tf_op jit(solution)/shard_map/pallas_call | solution.py:341
  64.0 0.8 %copy.7 = bf16[256,8,128]{2,1,0:T(8,128)(2,1)} copy(bf16[256,8,128]{2,1,0:T(8,128)(2,1)S(1)} %shard_map.55) | data formatting | bytes 1048576
Async XLA Ops:
  0.0 0.7 %copy-start.4 = (s32[1,2]{1,0:T(1,128)S(1)}, s32[1,2]{1,0:T(1,128)}, u32[]{:S(2)}) copy-start(s32[1,2]{1,0:T(1,128)} %heavy_in.1) | copy-start | bytes 28
  0.7 1.0 %copy-start = (bf16[256,8,128]{2,1,0:T(8,128)(2,1)S(1)}, bf16[256,8,128]{2,1,0:T(8,128)(2,1)}, u32[]{:S(2)}) copy-start(bf16[256,8,128]{2,1,0:T(8,128)(2,1)} %q_in.1) | copy-start | bytes 1572868
  1.7 1.0 %copy-start.1 = (bf16[256,8,128]{2,1,0:T(8,128)(2,1)S(1)}, bf16[256,8,128]{2,1,0:T(8,128)(2,1)}, u32[]{:S(2)}) copy-start(bf16[256,8,128]{2,1,0:T(8,128)(2,1)} %k_in.1) | copy-start | bytes 1572868
  2.7 1.0 %copy-start.2 = (bf16[256,8,128]{2,1,0:T(8,128)(2,1)S(1)}, bf16[256,8,128]{2,1,0:T(8,128)(2,1)}, u32[]{:S(2)}) copy-start(bf16[256,8,128]{2,1,0:T(8,128)(2,1)} %v_in.1) | copy-start | bytes 1572868
  3.8 0.7 %copy-start.3 = (s32[1,32,8]{1,2,0:T(8,128)S(1)}, s32[1,32,8]{1,2,0:T(8,128)}, u32[]{:S(2)}) copy-start(s32[1,32,8]{1,2,0:T(8,128)} %param.8) | copy-start | bytes 3076
